TPU v7x, 32 devices: a whole 2x2x4 slice. The times are simulated.
32 devices in a mesh: angle: 8 (over y, x, core), block: 4 (over z).
Axes of the slice: x: 2, y: 2, z: 4, core: 2. Of those that a mesh axis runs over, the one named last changes fastest.
Arguments:
- object_field: float32 [32, 2, 512, 512], P(None, None, 'block'), may hold values from -1.5 to 1.5
- shears: int32 [8, 32], P('angle'), may hold values from -16 to 16, as said below
- positions: int32 [8, 4, 2], P('angle', 'block'), may hold values from 0 to 511
- measured: bfloat16 [8, 4, 512, 512], P('angle', 'block'), may hold values from 0 to 2
- probe_field: float32 [2, 512, 512], replicated
- kappa_field: float32 [8, 512, 512], P('angle'), may hold values from 0.01 to 0.1
Outputs:
- updated_object: float32 [32, 2, 512, 512], P(None, None, 'block')
Inputs may be any that keep to these rules, and one draw needn't show every extreme that they name: `shears`: each angle's row offset of each slice; the values -16 and 16 occur in every draw.
All inputs are finite; a program needn't handle non-finite values.
Results may differ from a plain program's by a relative error of at most 0.0003.
Values sent between devices are 32-bit elements; how exact they have to be, the bound alone decides.
A program may use at most 192 MiB of HBM per device.

v0:
```python
import jax
import jax.numpy as jnp
from jax import lax
from jax.sharding import PartitionSpec as P

NX = 512
NY = 512
STEPS = 2
SH = 16


def with_halo(x, sides, width):
    for axis, dim in sides:
        count, length = (lax.axis_size(axis), x.shape[dim])
        up = [(i, (i + 1) % count) for i in range(count)]
        down = [(j, i) for i, j in up]
        last = lax.slice_in_dim(x, length - width, length, axis=dim)
        first = lax.slice_in_dim(x, 0, width, axis=dim)
        before = lax.ppermute(last, axis, up)
        after = lax.ppermute(first, axis, down)
        x = jnp.concatenate([before, x, after], axis=dim)
    return x


def laplace(field):
    return (
        jnp.roll(field, 1, -2)
        + jnp.roll(field, -1, -2)
        + jnp.roll(field, 1, -1)
        + jnp.roll(field, -1, -1)
        - 4.0 * field
    )


def frame_loss(projected, probe_field, kappa_row, offset, observed):
    window = jnp.roll(projected, (-offset[0], -offset[1]), axis=(1, 2))
    real_part = probe_field[0] * window[0] - probe_field[1] * window[1]
    imag_part = probe_field[0] * window[1] + probe_field[1] * window[0]
    for step in range(STEPS):
        real_part, imag_part = (
            real_part - kappa_row * laplace(imag_part),
            imag_part + kappa_row * laplace(real_part),
        )
    misfit = real_part * real_part + imag_part * imag_part - observed.astype(jnp.float32)
    return 0.5 * jnp.sum(misfit * misfit)


def per_device(object_field, shears, positions, measured, probe_field, kappa_field):
    strip_rows = object_field.shape[2]
    shear_row = shears[0]
    extended = with_halo(object_field, (("block", 2),), SH)

    def slice_rows(slab, amount):
        return lax.dynamic_slice_in_dim(slab, SH + amount, strip_rows, 1)

    own_strip = jnp.sum(jax.vmap(slice_rows)(extended, shear_row), axis=0)
    projected = lax.all_gather(own_strip, "block", axis=1, tiled=True)
    intensity = probe_field[0] * probe_field[0] + probe_field[1] * probe_field[1]
    kappa_row = kappa_field[0]

    def per_frame(totals, frame_in):
        offset, observed = frame_in
        grads = jax.grad(frame_loss)(projected, probe_field, kappa_row, offset, observed)
        weight = jnp.roll(intensity, (offset[0], offset[1]), axis=(0, 1))
        return (totals + jnp.concatenate([grads, weight[None]], 0), None)

    totals, _ = lax.scan(
        per_frame, jnp.zeros((3, NX, NY), jnp.float32), (positions[0], measured[0])
    )
    strip_totals = lax.psum_scatter(totals, "block", scatter_dimension=1, tiled=True)
    gradient_rim = with_halo(strip_totals, (("block", 1),), SH)

    def unshear_rows(rim_block, amount):
        return lax.dynamic_slice_in_dim(rim_block, SH - amount, strip_rows, 1)

    unsheared = jax.vmap(lambda amount: unshear_rows(gradient_rim, amount))(shear_row)
    summed = lax.psum(unsheared, "angle")
    return object_field - summed[:, :2] / (summed[:, 2:3] + 1.0)


def solution(mesh):
    placed = (
        P(None, None, "block", None),
        P("angle", None),
        P("angle", "block", None),
        P("angle", "block", None, None),
        P(),
        P("angle", None, None),
    )
    return jax.shard_map(
        per_device,
        mesh=mesh,
        in_specs=placed,
        out_specs=P(None, None, "block", None),
        check_vma=False,
    )
```

profile of v0, /device:TPU:0, one launch (start us, length us, event | category | flops | bytes accessed | tf_op | source)
XLA Modules:
  0.0 961.7 jit_solution(13056823166870190984)
XLA Ops:
  6.5 27.5 %copy.27 = f32[32,2,128,512]{3,1,0,2:T(2,128)S(1)} copy(f32[32,2,128,512]{3,2,1,0:T(8,128)} %param.6) | data formatting | bytes 33554432 | tf_op args[0]
  34.0 6.2 copy-done
  42.5 3.1 collective-permute-start
  47.7 46.4 %collective-permute-done = f32[32,2,16,512]{3,1,0,2:T(2,128)S(1)} collective-permute-done((f32[32,2,16,512]{3,1,0,2:T(2,128)S(1)}, f32[32,2,16,512]{3,1,0,2:T(2,128)S(1)}, u32[]{:S(2)}, u32[]{:S(2)}) %collective-permute-start) | collective-permute-done | bytes 2097184 | tf_op jit(solution)/shard_map/ppermute | solution.py:19
  94.1 43.5 %collective-permute-done.1 = f32[32,2,16,512]{3,1,0,2:T(2,128)S(1)} collective-permute-done((f32[32,2,16,512]{3,1,0,2:T(2,128)S(1)}, f32[32,2,16,512]{3,1,0,2:T(2,128)S(1)}, u32[]{:S(2)}, u32[]{:S(2)}) %collective-permute-start.1) | collective-permute-done | bytes 2097184 | tf_op jit(solution)/shard_map/ppermute | solution.py:20
  137.6 43.2 %pad_maximum_fusion = f32[32,2,160,512]{3,1,0,2:T(2,128)} fusion(f32[32,2,16,512]{3,1,0,2:T(2,128)S(1)} %collective-permute-done.1, f32[32,2,128,512]{3,1,0,2:T(2,128)} %copy-done, f32[32,2,16,512]{3,1,0,2:T(2,128)S(1)} %collective-permute-done), kind=kLoop, calls=%fused_computation.2 | loop fusion | flops 10485760 | bytes 41943040 | tf_op jit(solution)/shard_map/concatenate | solution.py:21
  180.7 27.7 %gather_fusion.1 = f32[32,2,128,512]{3,1,2,0:T(2,128)} fusion(f32[32,2,160,512]{3,1,0,2:T(2,128)} %pad_maximum_fusion, s32[32]{0:T(128)S(1)} %get-tuple-element.115), kind=kCustom, calls=%fused_computation.1 | custom fusion | bytes 33554944 | tf_op jit(solution)/shard_map/vmap()/gather | solution.py:54
  208.5 7.6 reduce_sum.9
  221.9 40.3 %all-gather.2.cloned.1.call-done = f32[2,512,512]{2,0,1:T(2,128)} async-done(((f32[2,128,512]{2,0,1:T(2,128)}), f32[2,512,512]{2,0,1:T(2,128)}) %all-gather.2.cloned.1.call-update) | async-done | bytes 2097168 | tf_op jit(solution)/shard_map/all_gather | solution.py:57
  262.2 5.6 fusion.3
  267.8 4.5 fusion.2
  276.1 12.8 %fusion.16 = (f32[512,512]{1,0:T(8,128)S(1)}, f32[512,512]{1,0:T(8,128)S(1)}) fusion(f32[511,512]{1,0:T(8,128)S(1)} %get-tuple-element.111, f32[1,512]{1,0:T(1,128)S(1)} %get-tuple-element.113, f32[1,512]{1,0:T(1,128)S(1)} %get-tuple-element.112, f32[511,512]{1,0:T(8,128)S(1)} %get-tuple-element.110, f32[512,511]{1,0:T(8,128)S(1)} %get-tuple-element.107, ...), kind=kLoop, calls=%fused_computation.36 | loop fusion | flops 3670016 | bytes 12582912 | tf_op jit(solution)/shard_map/while/body/eval_jaxpr/jvp()/sub | solution.py:41
  299.0 2.4 fusion.34
  306.0 3.1 broadcast_in_dim.37
  309.1 96.9 %dynamic_update_slice.10 = f32[2,512,1024]{2,0,1:T(2,128)} dynamic-update-slice(f32[2,512,1024]{2,0,1:T(2,128)} %broadcast_in_dim.37, f32[2,512,512]{2,0,1:T(2,128)S(1)} %copy.31, s32[]{:T(128)} %constant.100.clone.1, s32[]{:T(128)} %constant.100.clone.1, s32[]{:T(128)S(6)} %select_n.79) | dynamic-update-slice | bytes 4194308 | tf_op jit(solution)/shard_map/while/body/eval_jaxpr/transpose(jvp(jit(_roll_dynamic)))/dynamic_update_slice | solution.py:36
  412.3 3.9 pad_maximum_fusion.1
  418.2 151.9 %all-reduce.42.cloned.1.call-done = f32[3,512,512]{2,0,1:T(4,128)} async-done(((f32[3,512,512]{2,0,1:T(4,128)}), f32[3,512,512]{2,0,1:T(4,128)}) %all-reduce.42.cloned.1.call-update) | async-done | bytes 3145744
  571.2 3.8 collective-permute-start.3
  576.4 3.0 collective-permute-done.2
  579.6 21.4 %gather_fusion = f32[32,3,128,512]{3,1,2,0:T(4,128)} fusion(f32[3,160,512]{2,0,1:T(4,128)S(1)} %pad_maximum_fusion.2, s32[32]{0:T(128)S(1)} %get-tuple-element.114), kind=kCustom, calls=%fused_computation | custom fusion | bytes 50332032 | tf_op jit(solution)/shard_map/vmap()/gather | solution.py:74
  601.0 24.8 %copy.32 = f32[32,3,128,512]{3,2,1,0:T(8,128)} copy(f32[32,3,128,512]{3,1,2,0:T(4,128)} %gather_fusion) | data formatting | bytes 50331648 | tf_op jit(solution)/shard_map/vmap()/gather | solution.py:74
  625.9 307.4 %all-reduce.40.cloned.1.call-done = f32[32,3,128,512]{3,2,1,0:T(8,128)} async-done(((f32[32,3,128,512]{3,2,1,0:T(8,128)}), f32[32,3,128,512]{3,2,1,0:T(8,128)}) %all-reduce.40.cloned.1.call-update) | async-done | bytes 25165840 | tf_op jit(solution)/shard_map/psum | solution.py:77
  933.3 4.4 fusion.1
  937.7 17.0 %fusion = f32[32,2,128,512]{3,2,1,0:T(8,128)} fusion(f32[32,2,128,512]{3,2,1,0:T(8,128)} %param.6, f32[32,3,128,512]{3,2,1,0:T(8,128)} %all-reduce.40.cloned.1.call-done, f32[32,128,512]{2,1,0:T(8,128)S(1)} %fusion.1), kind=kLoop, calls=%fused_computation.4 | loop fusion | flops 8388608 | bytes 58720256 | tf_op jit(solution)/shard_map/sub | solution.py:78
  (76 shorter events, 33.9 us)
Async XLA Ops:
  6.5 255.6 %all-gather.2.cloned.1.call-start = ((), (), s32[]{:S(2)}) async-start(), calls=%async_computation | async-start | bytes 2621440 | tf_op jit(solution)/shard_map/all_gather | solution.py:57
  34.0 6.2 copy-start
  40.2 7.5 copy-start.6
  42.5 51.6 %collective-permute-start = (f32[32,2,16,512]{3,1,0,2:T(2,128)S(1)}, f32[32,2,16,512]{3,1,0,2:T(2,128)S(1)}, u32[]{:S(2)}, u32[]{:S(2)}) collective-permute-start(f32[32,2,16,512]{3,1,0,2:T(2,128)S(1)} %get-tuple-element.41), channel_id=1, source_target_pairs={{0,1},{1,2},{2,3},{3,0},{4,5},{5,6},{6,7},{7,4},{8,9},{9,10},{10,1... | collective-permute-start | bytes 6291464 | tf_op jit(solution)/shard_map/ppermute | solution.py:19
  45.5 92.0 %collective-permute-start.1 = (f32[32,2,16,512]{3,1,0,2:T(2,128)S(1)}, f32[32,2,16,512]{3,1,0,2:T(2,128)S(1)}, u32[]{:S(2)}, u32[]{:S(2)}) collective-permute-start(f32[32,2,16,512]{3,1,0,2:T(2,128)S(1)} %get-tuple-element.42), channel_id=1, source_target_pairs={{1,0},{2,1},{3,2},{0,3},{5,4},{6,5},{7,6},{4,7},{9,8},{10,9},{11,1... | collective-permute-start | bytes 6291464 | tf_op jit(solution)/shard_map/ppermute | solution.py:20
  208.4 7.9 copy-start.5
  216.1 354.0 %all-reduce.42.cloned.1.call-start = ((), (), s32[]{:S(2)}) async-start(), calls=%async_computation.2 | async-start | bytes 8388608
  272.3 1.6 copy-start.2
  274.8 1.2 copy-start.1
  291.7 1.0 copy-start.4
  405.9 2.2 copy-start.3
  416.2 0.7 copy-start.7
  416.2 517.0 %all-reduce.40.cloned.1.call-start = ((), (), s32[]{:S(2)}) async-start(), calls=%async_computation.1 | async-start | bytes 50331648 | tf_op jit(solution)/shard_map/psum | solution.py:77
  571.1 8.2 collective-permute-start.2
  571.2 8.2 collective-permute-start.3
Sparse Core Ops, SparseCore 0:
  216.2 45.9 all-gather.1
  416.3 153.6 all-reduce.41
  626.0 307.2 all-reduce.39
where the time goes:
time: 970 us; the launch traced here: 962 us
  waiting for transfers between devices  592 us (61%)
  local copies, waits for them, and re-layouts  228 us (24%)
  other arithmetic  113 us (12%)
  between operations  19.6 us (2%)
    psum x1, waiting for transfers between devices, per_device(): summed = lax.psum(unsheared, 'angle')  307 us
    unnamed x4, waiting for transfers between devices  152 us
    dynamic_update_slice x1, local copies, waits for them, and re-layouts, frame_loss(): window = jnp.roll(projected, (-offset[0], -offset[1]), axis=(1, 2))  96.9 us
    ppermute x2, waiting for transfers between devices, with_halo(): before = lax.ppermute(last, axis, up)  49.4 us
    gather x2, local copies, waits for them, and re-layouts, unshear_rows(): return lax.dynamic_slice_in_dim(rim_block, SH - amount, strip_rows, 1)  46.3 us
    ppermute x2, waiting for transfers between devices, with_halo(): after = lax.ppermute(first, axis, down)  43.5 us
    concatenate x2, other arithmetic, with_halo(): x = jnp.concatenate([before, x, after], axis=dim)  43.4 us
    all_gather x1, waiting for transfers between devices, per_device(): projected = lax.all_gather(own_strip, 'block', axis=1, tiled=True)  40.3 us
  transfers between devices with their start and end apart: 7, of which 6 were waited for; matrix products, arithmetic and copies ran while one was open for 0% of the time, Pallas kernels for 0%

commit v1 on v0

v1 whole, which is shorter than its diff:
```python
import functools
import jax
import jax.numpy as jnp
from jax import lax
from jax.experimental import pallas as pl
from jax.experimental.pallas import tpu as pltpu
from jax.sharding import PartitionSpec as P

NX = 512
NY = 512
STEPS = 2
SH = 16
EDGE = 24
LANES = 128
VMEM = pltpu.CompilerParams(vmem_limit_bytes=56 * 1024 * 1024)


def project_kernel(shears, field, out, padded):
    depth, rows = field.shape[0], field.shape[2]
    z0 = pl.program_id(1) * depth

    @pl.when(pl.program_id(1) == 0)
    def _():
        out[...] = jnp.zeros_like(out)
        zeros = jnp.zeros((depth, 2, 2 * SH, LANES), jnp.float32)
        padded[:, :, : 2 * SH] = zeros
        padded[:, :, 2 * SH + rows :] = zeros

    padded[:, :, 2 * SH : 2 * SH + rows] = field[...]
    for c in range(2):
        total = out[c]
        for z in range(depth):
            total = total + padded[z, c, pl.ds(SH + shears[0, z0 + z], rows + 2 * SH), :]
        out[c] = total


def project(shears, field):
    slices, _, rows, width = field.shape
    depth = 8
    return pl.pallas_call(
        project_kernel,
        out_shape=jax.ShapeDtypeStruct((2, rows + 2 * SH, width), jnp.float32),
        grid=(width // LANES, slices // depth),
        in_specs=[
            pl.BlockSpec(memory_space=pltpu.SMEM),
            pl.BlockSpec((depth, 2, rows, LANES), lambda i, j: (j, 0, 0, i)),
        ],
        out_specs=pl.BlockSpec((2, rows + 2 * SH, LANES), lambda i, j: (0, 0, i)),
        scratch_shapes=[pltpu.VMEM((depth, 2, rows + 4 * SH, LANES), jnp.float32)],
        compiler_params=VMEM,
        name="project",
    )(shears, field)


def spread(buffer, value, top):
    for j in range(NY // LANES):
        buffer[j, top : top + value.shape[0], :] = value[:, j * LANES : (j + 1) * LANES]


def rows_from(buffer, start, extent):
    parts = [buffer[j, pl.ds(start, extent), :] for j in range(NY // LANES)]
    return jnp.concatenate(parts, axis=1)


def shift_kernel(strips, positions, observed, out, wrapped):
    rows = NX // strips
    extent = rows + 2 * EDGE
    for f in range(observed.shape[0]):
        spread(wrapped, observed[f].astype(jnp.float32), 0)
        wrapped[:, NX:] = wrapped[:, :extent]
        p, q = positions[f, 0], positions[f, 1]
        for d in range(strips):
            start = lax.rem(d * rows - EDGE - p + 2 * NX, NX)
            out[d, f] = pltpu.roll(rows_from(wrapped, start, extent), q, 1)


def shift_measured(strips, positions, observed):
    extent = NX // strips + 2 * EDGE
    frames = observed.shape[0]
    return pl.pallas_call(
        functools.partial(shift_kernel, strips),
        out_shape=jax.ShapeDtypeStruct((strips, frames, extent, NY), jnp.float32),
        in_specs=[
            pl.BlockSpec(memory_space=pltpu.SMEM),
            pl.BlockSpec(memory_space=pltpu.VMEM),
        ],
        out_specs=pl.BlockSpec(memory_space=pltpu.VMEM),
        scratch_shapes=[pltpu.VMEM((NY // LANES, NX + extent, LANES), jnp.float32)],
        compiler_params=VMEM,
        name="shift_measured",
    )(positions, observed)


def laplace(field):
    rows, columns = field.shape
    return (
        pltpu.roll(field, 1, 0)
        + pltpu.roll(field, rows - 1, 0)
        + pltpu.roll(field, 1, 1)
        + pltpu.roll(field, columns - 1, 1)
        - 4.0 * field
    )


def frames_kernel(strip, positions, partial, before, after, observed, probe, kappa, out, wrapped, window):
    extent = window.shape[1]
    rows = extent - 2 * EDGE
    rim = EDGE - SH
    tall = EDGE + SH
    for i, source in enumerate((probe.at[0], probe.at[1], kappa)):
        spread(wrapped.at[i], source[...], 0)
        spread(wrapped.at[i], source[:extent], NX)
    window[:, :rim] = jnp.zeros((2, rim, NY), jnp.float32)
    window[:, rim + rows + 2 * SH :] = jnp.zeros((2, rim, NY), jnp.float32)
    window[:, rim : rim + rows + 2 * SH] = partial[...]
    window[:, :tall] += before[...]
    window[:, extent - tall :] += after[...]
    out[...] = jnp.zeros_like(out)

    @pl.loop(0, observed.shape[0])
    def _(f):
        p, q = positions[f, 0], positions[f, 1]
        start = lax.rem(strip[0] * rows - EDGE - p + 2 * NX, NX)

        def moved(i):
            return pltpu.roll(rows_from(wrapped.at[i], start, extent), q, 1)

        kappa_row = moved(2)
        probe_re, probe_im = moved(0), moved(1)
        re = probe_re * window[0] - probe_im * window[1]
        im = probe_re * window[1] + probe_im * window[0]
        for _ in range(STEPS):
            re, im = re - kappa_row * laplace(im), im + kappa_row * laplace(re)
        slope = 2.0 * (re * re + im * im - observed[f])
        re, im = slope * re, slope * im
        for _ in range(STEPS):
            re, im = re + laplace(kappa_row * im), im - laplace(kappa_row * re)
        keep = slice(rim, extent - rim)
        out[0] += (probe_re * re + probe_im * im)[keep]
        out[1] += (probe_re * im - probe_im * re)[keep]
        out[2] += (probe_re * probe_re + probe_im * probe_im)[keep]


def frame_gradients(strip, positions, partial, before, after, observed, probe, kappa):
    extent = observed.shape[1]
    smem = pl.BlockSpec(memory_space=pltpu.SMEM)
    vmem = pl.BlockSpec(memory_space=pltpu.VMEM)
    return pl.pallas_call(
        frames_kernel,
        out_shape=jax.ShapeDtypeStruct((3, extent - 2 * (EDGE - SH), NY), jnp.float32),
        in_specs=[smem, smem] + [vmem] * 6,
        out_specs=vmem,
        scratch_shapes=[
            pltpu.VMEM((3, NY // LANES, NX + extent, LANES), jnp.float32),
            pltpu.VMEM((2, extent, NY), jnp.float32),
        ],
        compiler_params=VMEM,
        name="frames",
    )(strip, positions, partial, before, after, observed, probe, kappa)


def update_kernel(shears, field, totals, out):
    depth, rows = field.shape[0], field.shape[2]
    angles = totals.shape[0]
    z0 = pl.program_id(1) * depth
    part = 64 if rows % 64 == 0 else rows

    @pl.loop(0, depth)
    def _(z):
        starts = [SH - shears[a, z0 + z] for a in range(angles)]
        for top in range(0, rows, part):

            def summed(c):
                terms = [totals[a, c, pl.ds(starts[a] + top, part), :] for a in range(angles)]
                return functools.reduce(jnp.add, terms)

            scale = 1.0 / (summed(2) + 1.0)
            for c in range(2):
                at = (z, c, pl.ds(top, part))
                out[at] = field[at] - summed(c) * scale


def update(shears, field, totals):
    slices, _, rows, width = field.shape
    angles, _, tall, _ = totals.shape
    depth = 4
    block = pl.BlockSpec((depth, 2, rows, LANES), lambda i, j: (j, 0, 0, i))
    return pl.pallas_call(
        update_kernel,
        out_shape=jax.ShapeDtypeStruct(field.shape, jnp.float32),
        grid=(width // LANES, slices // depth),
        in_specs=[
            pl.BlockSpec(memory_space=pltpu.SMEM),
            block,
            pl.BlockSpec((angles, 3, tall, LANES), lambda i, j: (0, 0, 0, i)),
        ],
        out_specs=block,
        compiler_params=VMEM,
        name="update",
    )(shears, field, totals)


def per_device(object_field, shears, positions, measured, probe_field, kappa_field):
    strips = lax.axis_size("block")
    rows = object_field.shape[2]
    frames = measured.shape[1]
    tall = EDGE + SH
    strip = lax.axis_index("block").reshape(1)
    all_positions = lax.all_gather(positions[0], "block", axis=0, tiled=True)
    all_shears = lax.all_gather(shears, "angle", axis=0, tiled=True)

    shifted = shift_measured(strips, positions[0], measured[0])
    observed = lax.all_to_all(shifted, "block", 0, 0, tiled=True)
    observed = observed.reshape(strips * frames, rows + 2 * EDGE, NY)

    partial = project(shears, object_field)
    up = [(i, (i + 1) % strips) for i in range(strips)]
    down = [(j, i) for i, j in up]
    before = lax.ppermute(partial[:, rows + 2 * SH - tall :], "block", up)
    after = lax.ppermute(partial[:, :tall], "block", down)

    totals = frame_gradients(
        strip, all_positions, partial, before, after, observed, probe_field, kappa_field[0]
    )
    gathered = lax.all_gather(totals, "angle", axis=0)
    return update(all_shears, object_field, gathered)


def solution(mesh):
    placed = (
        P(None, None, "block", None),
        P("angle", None),
        P("angle", "block", None),
        P("angle", "block", None, None),
        P(),
        P("angle", None, None),
    )
    return jax.shard_map(
        per_device,
        mesh=mesh,
        in_specs=placed,
        out_specs=P(None, None, "block", None),
        check_vma=False,
    )
```

time: 970 us -> 169 us (0.17)
  waiting for transfers between devices: 592 us -> 49.1 us
  local copies, waits for them, and re-layouts: 228 us -> 2.14 us
  other arithmetic: 113 us -> 0 us
  Pallas kernels: 0 us -> 64.2 us
  blocking collectives: 0 us -> 28.2 us
    psum x1 -> x0, waiting for transfers between devices: 307 us -> none  [per_device(): summed = lax.psum(unsheared, 'angle')]
    unnamed x4 -> x1, waiting for transfers between devices: 152 us -> 0.02 us
    dynamic_update_slice x1 -> x0, local copies, waits for them, and re-layouts: 96.9 us -> none  [frame_loss(): window = jnp.roll(projected, (-offset[0], -offset[1]), axis=(1, 2))]
    ppermute x4 -> x2, waiting for transfers between devices: 92.9 us -> 0.01 us  [the longest x1 0.01 us: per_device(): after = lax.ppermute(partial[:, :tall], 'block', down)]
    gather x3 -> x0, local copies, waits for them, and re-layouts: 74 us -> none  [the longest x2 46.3 us: unshear_rows(): return lax.dynamic_slice_in_dim(rim_block, SH - amount, strip_rows, 1)]
    pallas_call x0 -> x4, Pallas kernels: none -> 64.2 us  [the longest x1 34.9 us: update(): pl.pallas_call(update_kernel, out_shape=jax.ShapeDtypeStruct(field.shape,...]
    concatenate x8 -> x0, other arithmetic: 58.6 us -> none  [the longest x2 43.4 us: with_halo(): x = jnp.concatenate([before, x, after], axis=dim)]
    unnamed x19 -> x10, local copies, waits for them, and re-layouts: 39 us -> 1.11 us
  transfers between devices with their start and end apart: 7 -> 4, of which waited for: 6 -> 2; matrix products, arithmetic and copies ran while one was open for 0% -> 1% of each run, Pallas kernels for 0% -> 8%
where the time goes in v1:
time: 169 us; the launch traced here: 167 us
  Pallas kernels  64.2 us (38%)
  waiting for transfers between devices  49.1 us (29%)
  blocking collectives  28.2 us (17%)
  between operations  13.4 us (8%)
  starting transfers between devices  10.2 us (6%)
  local copies, waits for them, and re-layouts  2.14 us (1%)
    all_gather x1, waiting for transfers between devices, per_device(): gathered = lax.all_gather(totals, 'angle', axis=0)  46.7 us
    pallas_call x1, Pallas kernels, update(): pl.pallas_call(update_kernel, out_shape=jax.ShapeDtypeStruct(field.shape,...  34.9 us
    all_gather x1, blocking collectives, per_device(): all_positions = lax.all_gather(positions[0], 'block', axis=0, tiled=True)  18.4 us
    pallas_call x1, Pallas kernels, frame_gradients(): pl.pallas_call(frames_kernel, out_shape=jax.ShapeDtypeStruct((3, extent -...  13.7 us
    pallas_call x1, Pallas kernels, project(): pl.pallas_call(project_kernel, out_shape=jax.ShapeDtypeStruct((2, rows +...  13 us
    all_gather x1, blocking collectives, per_device(): all_shears = lax.all_gather(shears, 'angle', axis=0, tiled=True)  9.73 us
    all_to_all x1, starting transfers between devices, per_device(): observed = lax.all_to_all(shifted, 'block', 0, 0, tiled=True)  6.3 us
    ppermute x1, starting transfers between devices, per_device(): after = lax.ppermute(partial[:, :tall], 'block', down)  3.87 us
  transfers between devices with their start and end apart: 4, of which 2 were waited for; matrix products, arithmetic and copies ran while one was open for 1% of the time, Pallas kernels for 8%

profile of v1, /device:TPU:0, one launch (start us, length us, event | category | flops | bytes accessed | tf_op | source)
XLA Modules:
  0.0 167.2 jit_solution(14557935668670406147)
XLA Ops:
  6.5 2.7 %shift_measured.1 = f32[4,1,176,512]{3,2,1,0:T(8,128)} custom-call(s32[1,2]{1,0:T(1,128)} %bitcast.16, bf16[1,512,512]{2,1,0:T(8,128)(2,1)} %bitcast.12), custom_call_target="tpu_custom_call" | custom-call | tf_op jit(solution)/shard_map/shift_measured/pallas_call | solution.py:80
  9.3 6.3 %all-to-all-start = ((f32[4,1,176,512]{3,2,1,0:T(8,128)}), f32[4,1,176,512]{3,2,1,0:T(8,128)S(1)}, u32[]{:S(2)}, u32[]{:S(2)}) async-start(f32[4,1,176,512]{3,2,1,0:T(8,128)} %shift_measured.1), calls=%async_computation | async-start | bytes 2883584 | tf_op jit(solution)/shard_map/all_to_all | solution.py:213
  15.6 0.0 copy-start.4
  15.6 0.0 all-gather.5.cloned.1.call-start
  15.6 13.0 %project.1.partial = f32[2,160,512]{2,1,0:T(8,128)} custom-call(s32[1,32]{1,0:T(1,128)} %shears.1, f32[32,2,128,512]{3,2,1,0:T(8,128)} %field.3), custom_call_target="tpu_custom_call" | custom-call | tf_op jit(solution)/shard_map/project/pallas_call | solution.py:40
  28.5 1.0 fusion
  29.6 3.9 %collective-permute-start.1 = (f32[2,40,512]{2,1,0:T(8,128)S(1)}, f32[2,40,512]{2,1,0:T(8,128)S(1)}, u32[]{:S(2)}, u32[]{:S(2)}) collective-permute-start(f32[2,40,512]{2,1,0:T(8,128)S(1)} %get-tuple-element.5), channel_id=1, source_target_pairs={{1,0},{2,1},{3,2},{0,3},{5,4},{6,5},{7,6},{4,7},{9,8},{10,9},{11,1... | collective-permute-start | bytes 491528 | tf_op jit(solution)/shard_map/ppermute | solution.py:220
  33.5 0.0 collective-permute-start
  33.5 0.0 copy-done.4
  33.5 18.4 %all-gather = s32[4,1,2]{2,1,0:T(1,128)} all-gather(s32[1,1,2]{2,1,0:T(1,128)S(1)} %copy-done.4), channel_id=2, replica_groups=mesh['angle'=8,'block'=4] {'block'}, dimensions={0}, use_global_device_ids=true | all-gather | bytes 40 | tf_op jit(solution)/shard_map/all_gather | solution.py:209
  51.9 0.0 collective-permute-done.1.after
  51.9 0.0 copy-start.1
  51.9 0.0 collective-permute-done.before
  51.9 0.0 copy-start.2
  51.9 2.4 %all-to-all-done = f32[4,1,176,512]{3,2,1,0:T(8,128)S(1)} async-done(((f32[4,1,176,512]{3,2,1,0:T(8,128)}), f32[4,1,176,512]{3,2,1,0:T(8,128)S(1)}, u32[]{:S(2)}, u32[]{:S(2)}) %all-to-all-start) | async-done | bytes 1441824 | tf_op jit(solution)/shard_map/all_to_all | solution.py:213
  54.3 0.0 copy-done.1
  54.3 0.0 copy-done.2
  54.3 1.1 copy-done
  55.4 13.7 %frames.1 = f32[3,160,512]{2,1,0:T(8,128)} custom-call(s32[1]{0:T(128)} %bitcast.2.strip, s32[4,2]{1,0:T(4,128)} %bitcast.14, f32[2,160,512]{2,1,0:T(8,128)} %project.1.partial, f32[2,40,512]{2,1,0:T(8,128)} %copy-done.2, f32[2,40,512]{2,1,0:T(8,128)} %copy-done.1, f32[4,176,512]{2,1,0:T(8,128)} %bitcast.10, f32[2,512,512]{2,1,0:T(8,128)} %probe.1, ...), custom_call_target="tpu_custom_call" | custom-call | tf_op jit(solution)/shard_map/frames/pallas_call | solution.py:148
  69.1 0.0 all-gather.5.cloned.1.call-update
  69.1 0.0 copy-done.3
  69.1 9.7 %all-gather.2 = s32[8,1,32]{2,1,0:T(1,128)} all-gather(s32[1,1,32]{2,1,0:T(1,128)S(1)} %bitcast.15), channel_id=1, replica_groups=mesh['angle'=8,'block'=4] {'angle'}, dimensions={0}, use_global_device_ids=true | all-gather | bytes 1152 | tf_op jit(solution)/shard_map/all_gather | solution.py:210
  78.8 46.7 %all-gather.5.cloned.1.call-done = f32[24,160,512]{2,1,0:T(8,128)} async-done(((f32[3,160,512]{2,1,0:T(8,128)}), f32[24,160,512]{2,1,0:T(8,128)}) %all-gather.5.cloned.1.call-update) | async-done | bytes 7864336 | tf_op jit(solution)/shard_map/all_gather | solution.py:225
  125.5 34.9 %update.1 = f32[32,2,128,512]{3,2,1,0:T(8,128)} custom-call(s32[8,32]{1,0:T(8,128)} %bitcast.13, f32[32,2,128,512]{3,2,1,0:T(8,128)} %field.3, f32[8,3,160,512]{3,2,1,0:T(8,128)} %bitcast.9), custom_call_target="tpu_custom_call" | custom-call | tf_op jit(solution)/shard_map/update/pallas_call | solution.py:188
  (2 shorter events, 0.0 us)
Async XLA Ops:
  9.3 45.0 %all-to-all-start = ((f32[4,1,176,512]{3,2,1,0:T(8,128)}), f32[4,1,176,512]{3,2,1,0:T(8,128)S(1)}, u32[]{:S(2)}, u32[]{:S(2)}) async-start(f32[4,1,176,512]{3,2,1,0:T(8,128)} %shift_measured.1), calls=%async_computation | async-start | bytes 2883584 | tf_op jit(solution)/shard_map/all_to_all | solution.py:213
  15.6 17.9 %copy-start.4 = (s32[1,1,2]{2,1,0:T(1,128)S(1)}, s32[1,1,2]{2,1,0:T(1,128)}, u32[]{:S(2)}) copy-start(s32[1,1,2]{2,1,0:T(1,128)} %param.8) | copy-start | bytes 28
  15.6 110.0 %all-gather.5.cloned.1.call-start = ((), (), s32[]{:S(2)}) async-start(), calls=%async_computation.1 | async-start | bytes 8847360 | tf_op jit(solution)/shard_map/all_gather | solution.py:225
  28.5 40.5 %copy-start.3 = (s32[1,32]{1,0:T(1,128)S(1)}, s32[1,32]{1,0:T(1,128)}, u32[]{:S(2)}) copy-start(s32[1,32]{1,0:T(1,128)} %shears.1) | copy-start | bytes 388
  29.6 22.3 %collective-permute-start.1 = (f32[2,40,512]{2,1,0:T(8,128)S(1)}, f32[2,40,512]{2,1,0:T(8,128)S(1)}, u32[]{:S(2)}, u32[]{:S(2)}) collective-permute-start(f32[2,40,512]{2,1,0:T(8,128)S(1)} %get-tuple-element.5), channel_id=1, source_target_pairs={{1,0},{2,1},{3,2},{0,3},{5,4},{6,5},{7,6},{4,7},{9,8},{10,9},{11,1... | collective-permute-start | bytes 491528 | tf_op jit(solution)/shard_map/ppermute | solution.py:220
  33.5 18.4 %collective-permute-start = (f32[2,40,512]{2,1,0:T(8,128)S(1)}, f32[2,40,512]{2,1,0:T(8,128)S(1)}, u32[]{:S(2)}, u32[]{:S(2)}) collective-permute-start(f32[2,40,512]{2,1,0:T(8,128)S(1)} %get-tuple-element.6), channel_id=1, source_target_pairs={{0,1},{1,2},{2,3},{3,0},{4,5},{5,6},{6,7},{7,4},{8,9},{9,10},{10,1... | collective-permute-start | bytes 491528 | tf_op jit(solution)/shard_map/ppermute | solution.py:219
  51.9 2.4 %copy-start.1 = (f32[2,40,512]{2,1,0:T(8,128)}, f32[2,40,512]{2,1,0:T(8,128)S(1)}, u32[]{:S(2)}) copy-start(f32[2,40,512]{2,1,0:T(8,128)S(1)} %collective-permute-done.1.after) | copy-start | bytes 491524
  51.9 2.4 %copy-start.2 = (f32[2,40,512]{2,1,0:T(8,128)}, f32[2,40,512]{2,1,0:T(8,128)S(1)}, u32[]{:S(2)}) copy-start(f32[2,40,512]{2,1,0:T(8,128)S(1)} %collective-permute-done.before) | copy-start | bytes 491524
  54.3 1.1 copy-start
Sparse Core Ops, SparseCore 0:
  69.2 56.2 all-gather.4

commit v2 on v1

v2 whole, which is shorter than its diff:
```python
import functools
import jax
import jax.numpy as jnp
from jax import lax
from jax.experimental import pallas as pl
from jax.experimental.pallas import tpu as pltpu
from jax.sharding import PartitionSpec as P

NX = 512
NY = 512
STEPS = 2
SH = 16
EDGE = 24
LANES = 128
MESH = pl.DeviceIdType.MESH
VMEM = pltpu.CompilerParams(vmem_limit_bytes=56 * 1024 * 1024)


def spread(buffer, value, top):
    for j in range(NY // LANES):
        buffer[j, top : top + value.shape[0], :] = value[:, j * LANES : (j + 1) * LANES]


def rows_from(buffer, start, extent):
    parts = [buffer[j, pl.ds(start, extent), :] for j in range(NY // LANES)]
    return jnp.concatenate(parts, axis=1)


def exchange_kernel(
    strips, positions, shears, index_row, observed, field,
    shifted_out, index_out, partial_out, before_out, after_out,
    wrapped, stage, slab0, slab1, partial,
    local_sem, send_sem, recv_sem, index_send, index_recv, rim_send, rim_recv, slab_sem,
):
    me = lax.axis_index("block")
    frames = observed.shape[0]
    slices, _, rows, _ = field.shape
    extent = rows + 2 * EDGE
    tall = EDGE + SH
    blocks = NY // LANES
    depth = slab0.shape[1]

    def fetch(i, slab, slot, j):
        return pltpu.make_async_copy(
            field.at[pl.ds(i * depth, depth), :, :, pl.ds(j * LANES, LANES)],
            slab.at[j, :, :, pl.ds(2 * SH, rows), :],
            slab_sem.at[slot, j],
        )

    for j in range(blocks):
        fetch(0, slab0, 0, j).start()
        fetch(1, slab1, 1, j).start()

    barrier = pltpu.get_barrier_semaphore()
    for k in range(1, strips):
        peer = {"block": lax.rem(me + k, strips)}
        pl.semaphore_signal(barrier, inc=1, device_id=peer, device_id_type=MESH)

    for f in range(frames):
        spread(wrapped.at[f], observed[f].astype(jnp.float32), 0)
        wrapped[f, :, NX:] = wrapped[f, :, :extent]

    def shift(k):
        for f in range(frames):
            p, q = positions[f, 0], positions[f, 1]
            start = lax.rem(lax.rem(me + k, strips) * rows - EDGE - p + 2 * NX, NX)
            stage[k, f] = pltpu.roll(rows_from(wrapped.at[f], start, extent), q, 1)

    def ship(k, slot):
        return pltpu.make_async_remote_copy(
            src_ref=stage.at[k],
            dst_ref=shifted_out.at[slot],
            send_sem=send_sem.at[k],
            recv_sem=recv_sem.at[k],
            device_id={"block": lax.rem(me + k, strips)},
            device_id_type=MESH,
        )

    def ship_index(k, slot):
        return pltpu.make_async_remote_copy(
            src_ref=index_row,
            dst_ref=index_out.at[slot],
            send_sem=index_send.at[k],
            recv_sem=index_recv.at[k],
            device_id={"block": lax.rem(me + k, strips)},
            device_id_type=MESH,
        )

    order = sorted(range(1, strips), key=lambda k: abs(2 * k - strips))
    for n, k in enumerate(order):
        shift(k)
        if n == 0:
            pl.semaphore_wait(barrier, strips - 1)
        ship(k, me).start()
    for k in order:
        ship_index(k, me).start()
    shift(0)
    own = pltpu.make_async_copy(stage.at[0], shifted_out.at[me], local_sem.at[0])
    own_index = pltpu.make_async_copy(index_row, index_out.at[me], local_sem.at[1])
    own.start()
    own_index.start()

    zeros = jnp.zeros((depth, 2, 2 * SH, LANES), jnp.float32)
    for slab in (slab0, slab1):
        for j in range(blocks):
            slab[j, :, :, : 2 * SH] = zeros
            slab[j, :, :, 2 * SH + rows :] = zeros
    partial[...] = jnp.zeros_like(partial)
    rounds = slices // depth

    @pl.loop(0, rounds // 2)
    def _(pair):
        for slot, slab in enumerate((slab0, slab1)):
            i = 2 * pair + slot
            for j in range(blocks):
                fetch(i, slab, slot, j).wait()
            for j in range(blocks):
                for c in range(2):
                    total = partial[c, j]
                    for z in range(depth):
                        at = pl.ds(SH + shears[0, i * depth + z], rows + 2 * SH)
                        total = total + slab[j, z, c, at, :]
                    partial[c, j] = total

            @pl.when(pair < rounds // 2 - 1)
            def _():
                for j in range(blocks):
                    fetch(i + 2, slab, slot, j).start()

    def rim(side):
        step, top, landing = ((1, rows + 2 * SH - tall, before_out), (strips - 1, 0, after_out))[side]
        return pltpu.make_async_remote_copy(
            src_ref=partial.at[:, :, pl.ds(top, tall), :],
            dst_ref=landing,
            send_sem=rim_send.at[side],
            recv_sem=rim_recv.at[side],
            device_id={"block": lax.rem(me + step, strips)},
            device_id_type=MESH,
        )

    rim(0).start()
    rim(1).start()
    whole = pltpu.make_async_copy(partial, partial_out, local_sem.at[2])
    whole.start()
    own.wait()
    own_index.wait()
    whole.wait()
    for side in range(2):
        rim(side).wait()
    for k in order:
        source = lax.rem(me - k + strips, strips)
        ship_index(k, source).wait()
        ship(k, source).wait()


def exchange(strips, positions, shears, index_row, observed, field):
    slices, _, rows, _ = field.shape
    extent = rows + 2 * EDGE
    frames = observed.shape[0]
    blocks = NY // LANES
    depth = 4
    tall = EDGE + SH
    smem = pl.BlockSpec(memory_space=pltpu.SMEM)
    vmem = pl.BlockSpec(memory_space=pltpu.VMEM)
    anyw = pl.BlockSpec(memory_space=pl.ANY)
    f32 = jnp.float32
    slab = pltpu.VMEM((blocks, depth, 2, rows + 4 * SH, LANES), f32)
    dma = pltpu.SemaphoreType.DMA
    return pl.pallas_call(
        functools.partial(exchange_kernel, strips),
        out_shape=[
            jax.ShapeDtypeStruct((strips, frames, extent, NY), f32),
            jax.ShapeDtypeStruct((strips, 8, LANES), jnp.int32),
            jax.ShapeDtypeStruct((2, blocks, rows + 2 * SH, LANES), f32),
            jax.ShapeDtypeStruct((2, blocks, tall, LANES), f32),
            jax.ShapeDtypeStruct((2, blocks, tall, LANES), f32),
        ],
        in_specs=[smem, smem, vmem, vmem, anyw],
        out_specs=[anyw] * 5,
        scratch_shapes=[
            pltpu.VMEM((frames, blocks, NX + extent, LANES), f32),
            pltpu.VMEM((strips, frames, extent, NY), f32),
            slab,
            slab,
            pltpu.VMEM((2, blocks, rows + 2 * SH, LANES), f32),
            dma((3,)),
            dma((strips,)),
            dma((strips,)),
            dma((strips,)),
            dma((strips,)),
            dma((2,)),
            dma((2,)),
            dma((2, blocks)),
        ],
        compiler_params=pltpu.CompilerParams(
            vmem_limit_bytes=56 * 1024 * 1024, collective_id=0, has_side_effects=True
        ),
        name="exchange",
    )(positions, shears, index_row, observed, field)


def gather_kernel(
    held, totals, index_row, probe, out, index_out, weight,
    intensity, table, send_sem, recv_sem, index_send, index_recv, local_sem,
):
    angles = out.shape[0]
    me = lax.axis_index("angle")
    channels, tall = totals.shape[0], totals.shape[1]
    half = tall // 2
    core, x, y = lax.rem(me, 2), lax.rem(me // 2, 2), me // 4
    by_core = me + 1 - 2 * core
    by_x = me + 2 - 4 * x
    by_y = me + 4 - 8 * y
    corner = by_x + 4 - 8 * y

    barrier = pltpu.get_barrier_semaphore()
    for k in range(1, angles):
        peer = {"angle": lax.rem(me + k, angles)}
        pl.semaphore_signal(barrier, inc=1, device_id=peer, device_id_type=MESH)
    pl.semaphore_wait(barrier, angles - 1)

    def index_copy(k, slot):
        return pltpu.make_async_remote_copy(
            src_ref=index_row,
            dst_ref=index_out.at[slot],
            send_sem=index_send.at[k],
            recv_sem=index_recv.at[k],
            device_id={"angle": lax.rem(me + k, angles)},
            device_id_type=MESH,
        )

    def copy(kind, ch, source, owner, rows, target):
        return pltpu.make_async_remote_copy(
            src_ref=source.at[rows],
            dst_ref=out.at[owner, ch, rows],
            send_sem=send_sem.at[kind, ch],
            recv_sem=recv_sem.at[kind, ch],
            device_id={"angle": target},
            device_id_type=MESH,
        )

    every, first, second = pl.ds(0, tall), pl.ds(0, half), pl.ds(half, half)
    plan = (
        (every, by_x, me, by_x),
        (every, by_y, me, by_y),
        (every, by_core, me, by_core),
        (first, by_y, by_x, corner),
        (second, by_x, by_y, corner),
        (every, by_core, by_x, by_x + 1 - 2 * core),
        (every, by_core, by_y, by_y + 1 - 2 * core),
        (first, by_core, corner, corner + 1 - 2 * core),
        (second, by_core, corner, corner + 1 - 2 * core),
    )

    def begin(kind, ch):
        rows, target, owner, _ = plan[kind]
        source = totals.at[ch] if kind < 3 else out.at[owner, ch]
        copy(kind, ch, source, owner, rows, target).start()

    def landed(kind, ch):
        rows, target, _, owner = plan[kind]
        copy(kind, ch, totals.at[ch], owner, rows, target).wait_recv()

    for ch in range(channels):
        for kind in range(3):
            begin(kind, ch)
    for k in range(1, angles):
        index_copy(k, me).start()
    own = pltpu.make_async_copy(totals, out.at[me], local_sem.at[0])
    own_index = pltpu.make_async_copy(index_row, index_out.at[me], local_sem.at[1])
    own.start()
    own_index.start()
    square = probe[0] * probe[0] + probe[1] * probe[1]
    spread(intensity, square, 0)
    spread(intensity, square[:tall], NX)
    own_index.wait()
    for k in range(1, angles):
        index_copy(k, lax.rem(me - k + angles, angles)).wait()
    fill = pltpu.make_async_copy(index_out, table, local_sem.at[2])
    fill.start()
    fill.wait()
    strips = table.shape[1]
    first_row = lax.axis_index("block") * (tall - 2 * SH) - SH

    def weigh(low, high):
        @pl.loop(low, high)
        def _(a):
            total = jnp.zeros((tall, NY), jnp.float32)
            for b in range(strips):
                for f in range(held):
                    p, q = position(table.at[a, b], f)
                    start = lax.rem(first_row - p + 2 * NX, NX)
                    total = total + pltpu.roll(rows_from(intensity, start, tall), q, 1)
            weight[a] = total

    third = angles // 3
    weigh(0, third)
    for ch in range(channels):
        landed(0, ch)
        begin(3, ch)
        begin(5, ch)
        landed(1, ch)
        begin(4, ch)
        begin(6, ch)
    weigh(third, 2 * third)
    for ch in range(channels):
        landed(3, ch)
        begin(7, ch)
        landed(4, ch)
        begin(8, ch)
    weigh(2 * third, angles)
    own.wait()
    for ch in range(channels):
        for kind in (2, 5, 6, 7, 8):
            landed(kind, ch)
        for kind in range(9):
            rows, target, owner, _ = plan[kind]
            source = totals.at[ch] if kind < 3 else out.at[owner, ch]
            copy(kind, ch, source, owner, rows, target).wait_send()


def gather(angles, held, totals, index_row, probe):
    anyw = pl.BlockSpec(memory_space=pl.ANY)
    vmem = pl.BlockSpec(memory_space=pltpu.VMEM)
    dma = pltpu.SemaphoreType.DMA
    channels, tall, _ = totals.shape
    return pl.pallas_call(
        functools.partial(gather_kernel, held),
        out_shape=[
            jax.ShapeDtypeStruct((angles, *totals.shape), jnp.float32),
            jax.ShapeDtypeStruct((angles, *index_row.shape), jnp.int32),
            jax.ShapeDtypeStruct((angles, tall, NY), jnp.float32),
        ],
        in_specs=[anyw, anyw, vmem],
        out_specs=[anyw, anyw, vmem],
        scratch_shapes=[
            pltpu.VMEM((NY // LANES, NX + tall, LANES), jnp.float32),
            pltpu.SMEM((angles, *index_row.shape), jnp.int32),
            dma((9, channels)),
            dma((9, channels)),
            dma((angles,)),
            dma((angles,)),
            dma((3,)),
        ],
        compiler_params=pltpu.CompilerParams(
            vmem_limit_bytes=56 * 1024 * 1024, collective_id=1, has_side_effects=True
        ),
        name="gather",
    )(totals, index_row, probe)


def position(row, f):
    return row[0, LANES // 2 + 2 * f], row[0, LANES // 2 + 2 * f + 1]


def laplace(field):
    rows, columns = field.shape
    return (
        pltpu.roll(field, 1, 0)
        + pltpu.roll(field, rows - 1, 0)
        + pltpu.roll(field, 1, 1)
        + pltpu.roll(field, columns - 1, 1)
        - 4.0 * field
    )


def frames_kernel(strip, positions, partial, before, after, observed, probe, kappa, out, wrapped, window):
    extent = window.shape[1]
    rows = extent - 2 * EDGE
    rim = EDGE - SH
    tall = EDGE + SH
    for i, source in enumerate((probe.at[0], probe.at[1], kappa)):
        spread(wrapped.at[i], source[...], 0)
        spread(wrapped.at[i], source[:extent], NX)
    window[:, :rim] = jnp.zeros((2, rim, NY), jnp.float32)
    window[:, rim + rows + 2 * SH :] = jnp.zeros((2, rim, NY), jnp.float32)
    for j in range(NY // LANES):
        at = slice(j * LANES, (j + 1) * LANES)
        window[:, rim : rim + rows + 2 * SH, at] = partial[:, j]
        window[:, :tall, at] += before[:, j]
        window[:, extent - tall :, at] += after[:, j]
    out[...] = jnp.zeros_like(out)

    strips = positions.shape[0]
    held = observed.shape[0] // strips

    @pl.loop(0, observed.shape[0])
    def _(f):
        p, q = position(positions.at[f // held], lax.rem(f, held))
        start = lax.rem(strip[0] * rows - EDGE - p + 2 * NX, NX)

        def moved(i):
            return pltpu.roll(rows_from(wrapped.at[i], start, extent), q, 1)

        kappa_row = moved(2)
        probe_re, probe_im = moved(0), moved(1)
        re = probe_re * window[0] - probe_im * window[1]
        im = probe_re * window[1] + probe_im * window[0]
        for _ in range(STEPS):
            re, im = re - kappa_row * laplace(im), im + kappa_row * laplace(re)
        slope = 2.0 * (re * re + im * im - observed[f])
        re, im = slope * re, slope * im
        for _ in range(STEPS):
            re, im = re + laplace(kappa_row * im), im - laplace(kappa_row * re)
        keep = slice(rim, extent - rim)
        out[0] += (probe_re * re + probe_im * im)[keep]
        out[1] += (probe_re * im - probe_im * re)[keep]


def frame_gradients(strip, positions, partial, before, after, observed, probe, kappa):
    extent = observed.shape[1]
    smem = pl.BlockSpec(memory_space=pltpu.SMEM)
    vmem = pl.BlockSpec(memory_space=pltpu.VMEM)
    return pl.pallas_call(
        frames_kernel,
        out_shape=jax.ShapeDtypeStruct((2, extent - 2 * (EDGE - SH), NY), jnp.float32),
        in_specs=[smem, smem] + [vmem] * 6,
        out_specs=vmem,
        scratch_shapes=[
            pltpu.VMEM((3, NY // LANES, NX + extent, LANES), jnp.float32),
            pltpu.VMEM((2, extent, NY), jnp.float32),
        ],
        compiler_params=VMEM,
        name="frames",
    )(strip, positions, partial, before, after, observed, probe, kappa)


def update_kernel(shears, field, totals, weight, out):
    depth, rows = field.shape[0], field.shape[2]
    angles = totals.shape[0]
    z0 = pl.program_id(1) * depth
    part = 64 if rows % 64 == 0 else rows

    @pl.loop(0, depth)
    def _(z):
        starts = [SH - shears[a, z0 + z] for a in range(angles)]
        for top in range(0, rows, part):

            def summed(source):
                terms = [source(a)[pl.ds(starts[a] + top, part), :] for a in range(angles)]
                return functools.reduce(jnp.add, terms)

            scale = 1.0 / (summed(lambda a: weight.at[a]) + 1.0)
            for c in range(2):
                at = (z, c, pl.ds(top, part))
                out[at] = field[at] - summed(lambda a: totals.at[a, c]) * scale


def update(shears, field, totals, weight):
    slices, _, rows, width = field.shape
    angles, _, tall, _ = totals.shape
    depth = 4
    block = pl.BlockSpec((depth, 2, rows, LANES), lambda i, j: (j, 0, 0, i))
    return pl.pallas_call(
        update_kernel,
        out_shape=jax.ShapeDtypeStruct(field.shape, jnp.float32),
        grid=(width // LANES, slices // depth),
        in_specs=[
            pl.BlockSpec(memory_space=pltpu.SMEM),
            block,
            pl.BlockSpec((angles, 2, tall, LANES), lambda i, j: (0, 0, 0, i)),
            pl.BlockSpec((angles, tall, LANES), lambda i, j: (0, 0, i)),
        ],
        out_specs=block,
        compiler_params=VMEM,
        name="update",
    )(shears, field, totals, weight)


def per_device(object_field, shears, positions, measured, probe_field, kappa_field):
    strips = lax.axis_size("block")
    rows = object_field.shape[2]
    frames = measured.shape[1]
    strip = lax.axis_index("block").reshape(1)
    angles = lax.axis_size("angle")

    def half_row(values):
        flat = values.reshape(1, -1)
        return jnp.pad(flat, ((0, 7), (0, LANES // 2 - flat.shape[1])))

    index_row = jnp.concatenate([half_row(shears), half_row(positions)], axis=1)
    observed, index_rows, partial, before, after = exchange(
        strips, positions[0], shears, index_row, measured[0], object_field
    )
    observed = observed.reshape(strips * frames, rows + 2 * EDGE, NY)
    totals = frame_gradients(
        strip, index_rows, partial, before, after, observed, probe_field, kappa_field[0]
    )
    slices = object_field.shape[0]
    if angles == 8:
        gathered, table, weight = gather(angles, frames, totals, index_rows, probe_field)
        all_shears = table[:, 0, 0, :slices]
    else:
        gathered = lax.all_gather(totals, "angle", axis=0)
        all_shears = lax.all_gather(shears, "angle", axis=0, tiled=True)
        weight = weights_here(strip, index_rows, probe_field, rows)
        weight = lax.all_gather(weight, "angle", axis=0)
    return update(all_shears, object_field, gathered, weight)


def weights_here(strip, index_rows, probe_field, rows):
    intensity = probe_field[0] * probe_field[0] + probe_field[1] * probe_field[1]
    offsets = index_rows[:, 0, LANES // 2 : LANES // 2 + 2]
    total = 0.0
    for b in range(index_rows.shape[0]):
        top = SH - strip[0] * rows
        moved = jnp.roll(intensity, (offsets[b, 0] + top, offsets[b, 1]), axis=(0, 1))
        total = total + moved[: rows + 2 * SH]
    return total


def solution(mesh):
    placed = (
        P(None, None, "block", None),
        P("angle", None),
        P("angle", "block", None),
        P("angle", "block", None, None),
        P(),
        P("angle", None, None),
    )
    return jax.shard_map(
        per_device,
        mesh=mesh,
        in_specs=placed,
        out_specs=P(None, None, "block", None),
        check_vma=False,
    )
```

time: 169 us -> 138 us (0.82)
  Pallas kernels: 64.2 us -> 132 us
  waiting for transfers between devices: 49.1 us -> 0 us
  blocking collectives: 28.2 us -> 0 us
  between operations: 13.4 us -> 0.02 us
  starting transfers between devices: 10.2 us -> 0 us
    pallas_call x3, Pallas kernels: 29.4 us -> 97.8 us  [the longest x1 42.4 us: exchange(): pl.pallas_call(functools.partial(exchange_kernel, strips), out_shape=[jax...]
    all_gather x1 -> x0, waiting for transfers between devices: 46.7 us -> none  [per_device(): gathered = lax.all_gather(totals, 'angle', axis=0)]
    all_gather x2 -> x0, blocking collectives: 28.2 us -> none  [the longest x1 18.4 us: per_device(): all_positions = lax.all_gather(positions[0], 'block', axis=0, tiled=True)]
    all_to_all x1 -> x0, starting transfers between devices: 6.3 us -> none  [per_device(): observed = lax.all_to_all(shifted, 'block', 0, 0, tiled=True)]
    ppermute x2 -> x0, starting transfers between devices: 3.88 us -> none  [the longest x1 3.87 us: per_device(): after = lax.ppermute(partial[:, :tall], 'block', down)]
    all_to_all x1 -> x0, waiting for transfers between devices: 2.41 us -> none  [per_device(): observed = lax.all_to_all(shifted, 'block', 0, 0, tiled=True)]
  transfers between devices with their start and end apart: 4 -> 0, of which waited for: 2 -> 0; matrix products, arithmetic and copies ran while one was open for 1% -> 0% of each run, Pallas kernels for 8% -> 0%
where the time goes in v2:
time: 138 us; the launch traced here: 135 us
  Pallas kernels  132 us (96%)
  local copies, waits for them, and re-layouts  1.58 us (1%)
    pallas_call x1, Pallas kernels, exchange(): pl.pallas_call(functools.partial(exchange_kernel, strips), out_shape=[jax...  42.4 us
    pallas_call x1, Pallas kernels, gather(): pl.pallas_call(functools.partial(gather_kernel, held), out_shape=[jax.Sha...  42.2 us
    pallas_call x1, Pallas kernels, update(): pl.pallas_call(update_kernel, out_shape=jax.ShapeDtypeStruct(field.shape,...  34.7 us
    pallas_call x1, Pallas kernels, frame_gradients(): pl.pallas_call(frames_kernel, out_shape=jax.ShapeDtypeStruct((2, extent -...  13.3 us

profile of v2, /device:TPU:0, one launch (start us, length us, event | category | flops | bytes accessed | tf_op | source)
XLA Modules:
  0.0 135.4 jit_solution(4802366887965760506)
XLA Ops:
  0.0 1.3 pad_add_fusion.index_row
  1.3 42.4 %exchange.1 = (f32[4,1,176,512]{3,2,1,0:T(8,128)}, s32[4,8,128]{2,1,0:T(8,128)}, f32[2,4,160,128]{3,2,1,0:T(8,128)}, f32[2,4,40,128]{3,2,1,0:T(8,128)}, f32[2,4,40,128]{3,2,1,0:T(8,128)}) custom-call(s32[1,2]{1,0:T(1,128)} %bitcast.11, s32[1,32]{1,0:T(1,128)} %shears.1, s32[8,128]{1,0:T(8,128)} %pad_add_fusion.index_row, bf16[1,512,512]{2,1,0:T(8,128)(2,1)} %bitcast.9, ...), custom_call_target="tpu_custom_call" | custom-call | tf_op jit(solution)/shard_map/exchange/pallas_call | solution.py:169
  43.7 13.3 %frames.1.totals = f32[2,160,512]{2,1,0:T(8,128)} custom-call(s32[1]{0:T(128)} %bitcast.strip, s32[4,8,128]{2,1,0:T(8,128)} %get-tuple-element.13.positions.index_row, f32[2,4,160,128]{3,2,1,0:T(8,128)} %get-tuple-element.14.partial, f32[2,4,40,128]{3,2,1,0:T(8,128)} %get-tuple-element.15.before, f32[2,4,40,128]{3,2,1,0:T(8,128)} %get-tuple-element.16.after, ...), custom_call_target="tpu_custom_call" | custom-call | tf_op jit(solution)/shard_map/frames/pallas_call | solution.py:414
  57.0 42.2 %gather.1 = (f32[8,2,160,512]{3,2,1,0:T(8,128)}, s32[8,4,8,128]{3,2,1,0:T(8,128)}, f32[8,160,512]{2,1,0:T(8,128)}) custom-call(f32[2,160,512]{2,1,0:T(8,128)} %frames.1.totals, s32[4,8,128]{2,1,0:T(8,128)} %get-tuple-element.13.positions.index_row, f32[2,512,512]{2,1,0:T(8,128)} %probe.3), custom_call_target="tpu_custom_call" | custom-call | tf_op jit(solution)/shard_map/gather/pallas_call | solution.py:327
  99.2 1.0 copy.7
  100.1 0.6 slice_bitcast_fusion.shears
  100.7 34.7 %update.1 = f32[32,2,128,512]{3,2,1,0:T(8,128)} custom-call(s32[8,32]{1,0:T(8,128)} %slice_bitcast_fusion.shears, f32[32,2,128,512]{3,2,1,0:T(8,128)} %field.3, f32[8,2,160,512]{3,2,1,0:T(8,128)} %get-tuple-element.19.totals, f32[8,160,512]{2,1,0:T(8,128)} %get-tuple-element.20.weight), custom_call_target="tpu_custom_call" | custom-call | tf_op jit(solution)/shard_map/update/pallas_call | solution.py:454
